TPU v7x, 512 devices: a whole 4x4x16 slice. The times are simulated.
512 devices in a mesh: gx: 64 (over x, z), gy: 8 (over y, core).
Axes of the slice: x: 4, y: 4, z: 16, core: 2. Of those that a mesh axis runs over, the one named last changes fastest.
Arguments:
- snapshot: bfloat16 [3, 512, 128, 1024], P(None, 'gx', 'gy'), may hold values from -6 to 6
- basis: bfloat16 [3, 64, 16, 128, 512], P(None, 'gx', 'gy'), may hold values from -3000 to 3000
- taps: bfloat16 [3, 17], replicated, may hold values from 0.099609375 to 1
Outputs:
- new_modes: bfloat16 [3, 64, 16, 128, 512], P(None, 'gx', 'gy')
- new_mode: float32 [3, 64, 16, 128], P(None, 'gx', 'gy')
- factor: float32 [513, 513], replicated
All inputs are finite; a program needn't handle non-finite values.
Results may differ from a plain program's by a relative error of at most 0.0012.
The roundings to bfloat16 on the way count: a program that leaves them out, or rounds other values in their place, can miss the bound.
Values sent between devices are 32-bit elements; how exact they have to be, the bound alone decides.
A program may use at most 64 MiB of HBM per device.

v0:
```python
import jax
import jax.numpy as jnp
from jax import lax
from jax.sharding import PartitionSpec as P

STRIDE = 8


def padded(block, sides, width, periodic):
    for axis, dim in sides:
        count = lax.axis_size(axis)
        forward = [(i, i + 1) for i in range(count - 1)]
        if periodic:
            forward.append((count - 1, 0))
        backward = [(target, source) for source, target in forward]
        low = lax.ppermute(
            lax.slice_in_dim(block, block.shape[dim] - width, None, axis=dim), axis, forward
        )
        high = lax.ppermute(lax.slice_in_dim(block, 0, width, axis=dim), axis, backward)
        block = jnp.concatenate([low, block, high], axis=dim)
    return block


def band(taps_row, length, out_len, shift, wrap):
    rows = jnp.arange(length, dtype=jnp.int32)[:, None]
    cols = jnp.arange(out_len, dtype=jnp.int32)[None, :]
    lag = rows - STRIDE * cols + shift
    if wrap:
        lag = lag % length
    hits = lag[:, :, None] == jnp.arange(2 * STRIDE + 1, dtype=jnp.int32)[None, None, :]
    return jnp.sum(jnp.where(hits, taps_row[None, None, :], jnp.zeros((), taps_row.dtype)), axis=-1)


def local(snapshot, basis, taps):
    comps, cells_x, cells_y, cells_z = snapshot.shape
    modes = basis.shape[-1]
    flat_rows = basis.reshape(-1, modes)
    total = flat_rows.shape[0] * lax.axis_size("gx") * lax.axis_size("gy")
    matrix_z = band(taps[2], cells_z, cells_z // STRIDE, STRIDE, True)
    along_z = jnp.dot(snapshot.reshape(-1, cells_z), matrix_z, preferred_element_type=jnp.float32)
    along_z = along_z.reshape(comps, cells_x, cells_y, cells_z // STRIDE)
    padded_y = padded(along_z, (("gy", 2),), STRIDE, False)
    matrix_y = band(taps[1], cells_y + 2 * STRIDE, cells_y // STRIDE, 0, False).astype(jnp.float32)
    along_y = jnp.einsum("cxyz,yf->cxfz", padded_y, matrix_y, precision=lax.Precision.HIGHEST)
    padded_x = padded(along_y, (("gx", 1),), STRIDE, True)
    matrix_x = band(taps[0], cells_x + 2 * STRIDE, cells_x // STRIDE, 0, False).astype(jnp.float32)
    along_x = jnp.einsum("cxyz,xf->cfyz", padded_x, matrix_x, precision=lax.Precision.HIGHEST)
    filtered = along_x.astype(jnp.bfloat16).reshape(-1)
    stack = jnp.concatenate([flat_rows, filtered[:, None]], axis=1)
    gram = lax.psum(
        jnp.einsum("rk,rj->kj", stack, stack, preferred_element_type=jnp.float32), ("gx", "gy")
    )
    gram = gram / total
    lower = jnp.linalg.cholesky(gram)
    solved = lax.linalg.triangular_solve(
        lower, stack.astype(jnp.float32), left_side=False, lower=True, transpose_a=True
    )
    new_modes = solved[:, :modes].astype(jnp.bfloat16).reshape(basis.shape)
    new_mode = solved[:, modes].reshape(basis.shape[:-1])
    return (new_modes, new_mode, lower.T)


def solution(mesh):
    in_specs = (P(None, "gx", "gy", None), P(None, "gx", "gy", None, None), P())
    out_specs = (P(None, "gx", "gy", None, None), P(None, "gx", "gy", None), P())
    return jax.shard_map(local, mesh=mesh, in_specs=in_specs, out_specs=out_specs, check_vma=False)
```

profile of v0, /device:TPU:1, one launch (start us, length us, event | category | flops | bytes accessed | tf_op | source)
XLA Modules:
  0.0 709.4 jit_solution(6518800129823269705)
XLA Ops:
  9.8 4.6 collective-permute-start
  14.4 5.5 collective-permute-start.1
  21.1 3.1 collective-permute-start.2
  24.1 11.7 %collective-permute-start.3 = (f32[3,8,2,128]{3,2,1,0:T(2,128)S(1)}, f32[3,8,2,128]{3,2,1,0:T(2,128)S(1)}, u32[]{:S(2)}, u32[]{:S(2)}) collective-permute-start(f32[3,8,2,128]{3,2,1,0:T(2,128)S(1)} %convolution_bitcast_fusion.1), channel_id=1, source_target_pairs={{8,0},{16,8},{24,16},{32,24},{40,32},{48,40},{56,48},{64,56},{72,6... | collective-permute-start | bytes 73736 | tf_op jit(solution)/shard_map/ppermute | solution.py:19
  40.7 462.9 %all-reduce.5.cloned.1.call-done = f32[513,513]{0,1:T(8,128)} async-done(((f32[513,513]{0,1:T(8,128)}), f32[513,513]{0,1:T(8,128)}) %all-reduce.5.cloned.1.call-update) | async-done | bytes 1052692 | tf_op jit(solution)/shard_map/psum | solution.py:50
  503.6 2.5 broadcast_multiply_fusion
  509.8 11.7 %cholesky.131 = f32[128,128]{1,0:T(8,128)S(1)} custom-call(f32[128,128]{1,0:T(8,128)S(1)} %cholesky.333), custom_call_target="Cholesky" | custom-call | tf_op jit(solution)/shard_map/jit(cholesky)/cholesky | solution.py:54
  521.6 9.8 %custom-call.35 = f32[1,128,128]{1,2,0:T(8,128)S(1)} custom-call(f32[1,128,128]{2,1,0:T(8,128)S(1)} %get-tuple-element.47), custom_call_target="InvertDiagBlocksLowerTriangular" | custom-call | tf_op jit(solution)/shard_map/jit(cholesky)/cholesky | solution.py:54
  534.3 11.9 %cholesky.264 = f32[128,128]{1,0:T(8,128)S(1)} custom-call(f32[128,128]{1,0:T(8,128)S(1)} %cholesky.337), custom_call_target="Cholesky" | custom-call | tf_op jit(solution)/shard_map/jit(cholesky)/cholesky | solution.py:54
  546.2 9.8 %custom-call.36 = f32[1,128,128]{1,2,0:T(8,128)S(1)} custom-call(f32[1,128,128]{2,1,0:T(8,128)S(1)} %get-tuple-element.44), custom_call_target="InvertDiagBlocksLowerTriangular" | custom-call | tf_op jit(solution)/shard_map/jit(cholesky)/cholesky | solution.py:54
  557.7 11.7 %cholesky.285 = f32[128,128]{1,0:T(8,128)S(1)} custom-call(f32[128,128]{1,0:T(8,128)S(1)} %cholesky.342), custom_call_target="Cholesky" | custom-call | tf_op jit(solution)/shard_map/jit(cholesky)/cholesky | solution.py:54
  569.5 9.8 %custom-call.37 = f32[1,128,128]{1,2,0:T(8,128)S(1)} custom-call(f32[1,128,128]{2,1,0:T(8,128)S(1)} %get-tuple-element.41), custom_call_target="InvertDiagBlocksLowerTriangular" | custom-call | tf_op jit(solution)/shard_map/jit(cholesky)/cholesky | solution.py:54
  580.8 11.9 %cholesky.304 = f32[128,128]{1,0:T(8,128)S(1)} custom-call(f32[128,128]{1,0:T(8,128)S(1)} %cholesky.347), custom_call_target="Cholesky" | custom-call | tf_op jit(solution)/shard_map/jit(cholesky)/cholesky | solution.py:54
  592.8 9.8 %custom-call.38 = f32[1,128,128]{1,2,0:T(8,128)S(1)} custom-call(f32[1,128,128]{2,1,0:T(8,128)S(1)} %get-tuple-element.38), custom_call_target="InvertDiagBlocksLowerTriangular" | custom-call | tf_op jit(solution)/shard_map/jit(cholesky)/cholesky | solution.py:54
  611.3 10.1 %while.1 = (s32[]{:T(128)}, f32[513,513]{1,0:T(8,128)S(1)}, s32[4,2]{0,1:T(2,128)S(1)}, f32[4,128,128]{2,1,0:T(8,128)}, s32[]{:T(128)}) while((s32[]{:T(128)}, f32[513,513]{1,0:T(8,128)S(1)}, s32[4,2]{0,1:T(2,128)S(1)}, f32[4,128,128]{2,1,0:T(8,128)}, s32[]{:T(128)}) %tuple.44), condition=%wide.while_cond, body=%wide.while_body.sunk | while | flops 2 | bytes 132705 | solution.py:55
  623.1 49.1 %custom-call.39 = f32[5,128,128]{1,2,0:T(8,128)S(1)} custom-call(f32[5,128,128]{2,1,0:T(8,128)S(1)} %pad_maximum_fusion.3), custom_call_target="InvertDiagBlocksLowerTriangular" | custom-call | tf_op jit(solution)/shard_map/triangular_solve | solution.py:55
  672.2 2.1 bitcast_convert_fusion
  676.8 2.1 fusion.73
  680.1 2.3 convolution_subtract_fusion.2
  682.4 2.1 fusion.72
  686.4 3.1 convolution_subtract_fusion
  689.5 2.1 fusion.71
  693.5 2.0 fusion.17
  698.2 2.9 copy.69
  (100 shorter events, 46.0 us)
Async XLA Ops:
  7.2 2.1 copy-start
  7.2 496.4 %all-reduce.5.cloned.1.call-start = ((), (), s32[]{:S(2)}) async-start(), calls=%async_computation | async-start | bytes 2662400 | tf_op jit(solution)/shard_map/psum | solution.py:50
  9.2 28.1 %copy-start.5 = (bf16[3,1,2,128,512]{4,3,2,1,0:T(8,128)(2,1)S(1)}, bf16[3,1,2,128,512]{4,3,2,1,0:T(8,128)(2,1)}, u32[]{:S(2)}) copy-start(bf16[3,1,2,128,512]{4,3,2,1,0:T(8,128)(2,1)} %param.4) | copy-start | bytes 2359300
  9.8 10.3 %collective-permute-start = (f32[3,8,8,128]{3,2,1,0:T(8,128)S(1)}, f32[3,8,8,128]{3,2,1,0:T(8,128)S(1)}, u32[]{:S(2)}, u32[]{:S(2)}) collective-permute-start(f32[3,8,8,128]{3,2,1,0:T(8,128)S(1)} %get-tuple-element.35), channel_id=1, source_target_pairs={{0,1},{1,2},{2,3},{3,4},{4,5},{5,6},{6,7},{8,9},{9,10},{10,11},{11... | collective-permute-start | bytes 294920 | tf_op jit(solution)/shard_map/ppermute | solution.py:16
  14.4 6.4 collective-permute-start.1
  21.1 14.9 %collective-permute-start.2 = (f32[3,8,2,128]{3,2,1,0:T(2,128)S(1)}, f32[3,8,2,128]{3,2,1,0:T(2,128)S(1)}, u32[]{:S(2)}, u32[]{:S(2)}) collective-permute-start(f32[3,8,2,128]{3,2,1,0:T(2,128)S(1)} %convolution_bitcast_fusion.1), channel_id=1, source_target_pairs={{0,8},{8,16},{16,24},{24,32},{32,40},{40,48},{48,56},{56,64},{64,7... | collective-permute-start | bytes 73736 | tf_op jit(solution)/shard_map/ppermute | solution.py:16
  24.1 12.6 %collective-permute-start.3 = (f32[3,8,2,128]{3,2,1,0:T(2,128)S(1)}, f32[3,8,2,128]{3,2,1,0:T(2,128)S(1)}, u32[]{:S(2)}, u32[]{:S(2)}) collective-permute-start(f32[3,8,2,128]{3,2,1,0:T(2,128)S(1)} %convolution_bitcast_fusion.1), channel_id=1, source_target_pairs={{8,0},{16,8},{24,16},{32,24},{40,32},{48,40},{56,48},{64,56},{72,6... | collective-permute-start | bytes 73736 | tf_op jit(solution)/shard_map/ppermute | solution.py:19
  506.1 1.9 copy-start.2
  508.2 1.1 copy-start.4
  621.4 53.5 %copy-start.3 = (f32[513,513]{1,0:T(8,128)}, f32[513,513]{1,0:T(8,128)S(1)}, u32[]{:S(2)}) copy-start(f32[513,513]{1,0:T(8,128)S(1)} %get-tuple-element.109) | copy-start | bytes 3158032
  672.2 2.6 copy-start.9
  674.8 5.2 copy-start.1
  698.2 3.0 copy-start.6
  698.2 2.9 copy-start.7
  698.2 2.9 copy-start.8
Sparse Core Ops, SparseCore 0:
  39.4 464.2 all-reduce.4
where the time goes:
time: 720 us; the launch traced here: 709 us
  waiting for transfers between devices  464 us (64%)
  other arithmetic  149 us (21%)
  matrix products  26.7 us (4%)
  local copies, waits for them, and re-layouts  25.8 us (4%)
  starting transfers between devices  24.9 us (3%)
  between operations  18.8 us (3%)
    psum x1, waiting for transfers between devices, local(): lax.psum(jnp.einsum('rk,rj->kj', stack, stack, preferred_element_type=jnp...  463 us
    another operation x16, other arithmetic, local(): lower = jnp.linalg.cholesky(gram)  89.2 us
    another operation x8, other arithmetic, local(): lax.linalg.triangular_solve(lower, stack.astype(jnp.float32), left_side=F...  52.8 us
    another operation x8, matrix products, local(): lax.linalg.triangular_solve(lower, stack.astype(jnp.float32), left_side=F...  17.8 us
    ppermute x2, starting transfers between devices, padded(): lax.ppermute(lax.slice_in_dim(block, 0, width, axis=dim), axis, backward)  17.2 us
  transfers between devices with their start and end apart: 5, of which 3 were waited for; matrix products, arithmetic and copies ran while one was open for 0% of the time, Pallas kernels for 0%

commit v1 on v0

--- a/solution.py
+++ b/solution.py
@@ -48,7 +48,8 @@
     filtered = along_x.astype(jnp.bfloat16).reshape(-1)
     stack = jnp.concatenate([flat_rows, filtered[:, None]], axis=1)
     gram = lax.psum(
-        jnp.einsum("rk,rj->kj", stack, stack, preferred_element_type=jnp.float32), ("gx", "gy")
+        lax.psum(jnp.einsum("rk,rj->kj", stack, stack, preferred_element_type=jnp.float32), "gy"),
+        "gx",
     )
     gram = gram / total
     lower = jnp.linalg.cholesky(gram)

time: 720 us -> 602 us (0.84)
  the two profiles are of different devices: /device:TPU:1 before, /device:TPU:8 now
where the time goes in v1:
time: 602 us; the launch traced here: 598 us
  waiting for transfers between devices  356 us (59%)
  other arithmetic  149 us (25%)
  matrix products  26.7 us (4%)
  local copies, waits for them, and re-layouts  26.2 us (4%)
  starting transfers between devices  21.6 us (4%)
  between operations  18.6 us (3%)
    psum x1, waiting for transfers between devices, local(): lax.psum(lax.psum(jnp.einsum('rk,rj->kj', stack, stack, preferred_element...  280 us
    another operation x16, other arithmetic, local(): lower = jnp.linalg.cholesky(gram)  89.2 us
    psum x1, waiting for transfers between devices, local(): lax.psum(jnp.einsum('rk,rj->kj', stack, stack, preferred_element_type=jnp...  73.1 us
    another operation x8, other arithmetic, local(): lax.linalg.triangular_solve(lower, stack.astype(jnp.float32), left_side=F...  52.8 us
    another operation x8, matrix products, local(): lax.linalg.triangular_solve(lower, stack.astype(jnp.float32), left_side=F...  17.8 us
    ppermute x2, starting transfers between devices, padded(): lax.ppermute(lax.slice_in_dim(block, 0, width, axis=dim), axis, backward)  15.3 us
  transfers between devices with their start and end apart: 6, of which 5 were waited for; matrix products, arithmetic and copies ran while one was open for 0% of the time, Pallas kernels for 0%

profile of v1, /device:TPU:8, one launch (start us, length us, event | category | flops | bytes accessed | tf_op | source)
XLA Modules:
  0.0 598.3 jit_solution(12461514328360084883)
XLA Ops:
  11.7 3.6 collective-permute-start.1
  17.8 3.8 collective-permute-start.2
  21.6 11.7 %collective-permute-start.3 = (f32[3,8,2,128]{3,2,1,0:T(2,128)S(1)}, f32[3,8,2,128]{3,2,1,0:T(2,128)S(1)}, u32[]{:S(2)}, u32[]{:S(2)}) collective-permute-start(f32[3,8,2,128]{3,2,1,0:T(2,128)S(1)} %convolution_bitcast_fusion.1), channel_id=1, source_target_pairs={{8,0},{16,8},{24,16},{32,24},{40,32},{48,40},{56,48},{64,56},{72,6... | collective-permute-start | bytes 73736 | tf_op jit(solution)/shard_map/ppermute | solution.py:19
  37.8 73.1 %all-reduce.6.cloned.1.call-done = f32[513,513]{0,1:T(8,128)} async-done(((f32[513,513]{0,1:T(8,128)}), f32[513,513]{0,1:T(8,128)}) %all-reduce.6.cloned.1.call-update) | async-done | bytes 1052692 | tf_op jit(solution)/shard_map/psum | solution.py:51
  112.4 279.8 %all-reduce.8.cloned.1.call-done = f32[513,513]{0,1:T(8,128)} async-done(((f32[513,513]{0,1:T(8,128)}), f32[513,513]{0,1:T(8,128)}) %all-reduce.8.cloned.1.call-update) | async-done | bytes 1052692 | tf_op jit(solution)/shard_map/psum | solution.py:50
  392.3 2.5 broadcast_multiply_fusion
  398.5 11.7 %cholesky.131 = f32[128,128]{1,0:T(8,128)S(1)} custom-call(f32[128,128]{1,0:T(8,128)S(1)} %cholesky.333), custom_call_target="Cholesky" | custom-call | tf_op jit(solution)/shard_map/jit(cholesky)/cholesky | solution.py:55
  410.2 9.8 %custom-call.35 = f32[1,128,128]{1,2,0:T(8,128)S(1)} custom-call(f32[1,128,128]{2,1,0:T(8,128)S(1)} %get-tuple-element.47), custom_call_target="InvertDiagBlocksLowerTriangular" | custom-call | tf_op jit(solution)/shard_map/jit(cholesky)/cholesky | solution.py:55
  423.0 11.7 %cholesky.264 = f32[128,128]{1,0:T(8,128)S(1)} custom-call(f32[128,128]{1,0:T(8,128)S(1)} %cholesky.337), custom_call_target="Cholesky" | custom-call | tf_op jit(solution)/shard_map/jit(cholesky)/cholesky | solution.py:55
  434.7 9.9 %custom-call.36 = f32[1,128,128]{1,2,0:T(8,128)S(1)} custom-call(f32[1,128,128]{2,1,0:T(8,128)S(1)} %get-tuple-element.44), custom_call_target="InvertDiagBlocksLowerTriangular" | custom-call | tf_op jit(solution)/shard_map/jit(cholesky)/cholesky | solution.py:55
  446.3 11.7 %cholesky.285 = f32[128,128]{1,0:T(8,128)S(1)} custom-call(f32[128,128]{1,0:T(8,128)S(1)} %cholesky.342), custom_call_target="Cholesky" | custom-call | tf_op jit(solution)/shard_map/jit(cholesky)/cholesky | solution.py:55
  458.1 9.8 %custom-call.37 = f32[1,128,128]{1,2,0:T(8,128)S(1)} custom-call(f32[1,128,128]{2,1,0:T(8,128)S(1)} %get-tuple-element.41), custom_call_target="InvertDiagBlocksLowerTriangular" | custom-call | tf_op jit(solution)/shard_map/jit(cholesky)/cholesky | solution.py:55
  469.5 11.9 %cholesky.304 = f32[128,128]{1,0:T(8,128)S(1)} custom-call(f32[128,128]{1,0:T(8,128)S(1)} %cholesky.347), custom_call_target="Cholesky" | custom-call | tf_op jit(solution)/shard_map/jit(cholesky)/cholesky | solution.py:55
  481.4 9.8 %custom-call.38 = f32[1,128,128]{1,2,0:T(8,128)S(1)} custom-call(f32[1,128,128]{2,1,0:T(8,128)S(1)} %get-tuple-element.38), custom_call_target="InvertDiagBlocksLowerTriangular" | custom-call | tf_op jit(solution)/shard_map/jit(cholesky)/cholesky | solution.py:55
  499.9 10.6 %while.1 = (s32[]{:T(128)}, f32[513,513]{1,0:T(8,128)S(1)}, s32[4,2]{0,1:T(2,128)S(1)}, f32[4,128,128]{2,1,0:T(8,128)}, s32[]{:T(128)}) while((s32[]{:T(128)}, f32[513,513]{1,0:T(8,128)S(1)}, s32[4,2]{0,1:T(2,128)S(1)}, f32[4,128,128]{2,1,0:T(8,128)}, s32[]{:T(128)}) %tuple.44), condition=%wide.while_cond, body=%wide.while_body.sunk | while | flops 2 | bytes 132705 | solution.py:56
  512.2 49.1 %custom-call.39 = f32[5,128,128]{1,2,0:T(8,128)S(1)} custom-call(f32[5,128,128]{2,1,0:T(8,128)S(1)} %pad_maximum_fusion.3), custom_call_target="InvertDiagBlocksLowerTriangular" | custom-call | tf_op jit(solution)/shard_map/triangular_solve | solution.py:56
  561.3 2.1 bitcast_convert_fusion
  565.9 2.1 fusion.73
  569.2 2.3 convolution_subtract_fusion.2
  571.5 2.1 fusion.72
  575.5 3.1 convolution_subtract_fusion
  578.6 2.1 fusion.71
  582.7 2.0 fusion.17
  587.4 2.9 copy.69
  (103 shorter events, 50.8 us)
Async XLA Ops:
  7.2 2.1 copy-start
  7.2 103.7 %all-reduce.6.cloned.1.call-start = ((), (), s32[]{:S(2)}) async-start(), calls=%async_computation | async-start | bytes 2662400 | tf_op jit(solution)/shard_map/psum | solution.py:51
  9.2 26.2 %copy-start.5 = (bf16[3,1,2,128,512]{4,3,2,1,0:T(8,128)(2,1)S(1)}, bf16[3,1,2,128,512]{4,3,2,1,0:T(8,128)(2,1)}, u32[]{:S(2)}) copy-start(bf16[3,1,2,128,512]{4,3,2,1,0:T(8,128)(2,1)} %param.4) | copy-start | bytes 2359300
  9.8 5.9 collective-permute-start
  11.7 5.8 collective-permute-start.1
  17.8 15.7 %collective-permute-start.2 = (f32[3,8,2,128]{3,2,1,0:T(2,128)S(1)}, f32[3,8,2,128]{3,2,1,0:T(2,128)S(1)}, u32[]{:S(2)}, u32[]{:S(2)}) collective-permute-start(f32[3,8,2,128]{3,2,1,0:T(2,128)S(1)} %convolution_bitcast_fusion.1), channel_id=1, source_target_pairs={{0,8},{8,16},{16,24},{24,32},{32,40},{40,48},{48,56},{56,64},{64,7... | collective-permute-start | bytes 73736 | tf_op jit(solution)/shard_map/ppermute | solution.py:16
  21.6 13.2 %collective-permute-start.3 = (f32[3,8,2,128]{3,2,1,0:T(2,128)S(1)}, f32[3,8,2,128]{3,2,1,0:T(2,128)S(1)}, u32[]{:S(2)}, u32[]{:S(2)}) collective-permute-start(f32[3,8,2,128]{3,2,1,0:T(2,128)S(1)} %convolution_bitcast_fusion.1), channel_id=1, source_target_pairs={{8,0},{16,8},{24,16},{32,24},{40,32},{48,40},{56,48},{64,56},{72,6... | collective-permute-start | bytes 73736 | tf_op jit(solution)/shard_map/ppermute | solution.py:19
  37.3 354.9 %all-reduce.8.cloned.1.call-start = ((), (), s32[]{:S(2)}) async-start(), calls=%async_computation.1 | async-start | bytes 2662400 | tf_op jit(solution)/shard_map/psum | solution.py:50
  394.8 1.9 copy-start.2
  396.9 1.1 copy-start.4
  510.5 53.5 %copy-start.3 = (f32[513,513]{1,0:T(8,128)}, f32[513,513]{1,0:T(8,128)S(1)}, u32[]{:S(2)}) copy-start(f32[513,513]{1,0:T(8,128)S(1)} %get-tuple-element.110) | copy-start | bytes 3158032
  561.3 2.6 copy-start.9
  564.0 5.2 copy-start.1
  587.3 3.0 copy-start.6
  587.3 2.9 copy-start.7
  587.3 2.9 copy-start.8
Sparse Core Ops, SparseCore 0:
  37.4 73.4 all-reduce.5
  114.7 277.5 all-reduce.7
